TPU v7x, 256 devices: a whole 4x4x8 slice. The times are simulated.
256 devices in a mesh: dp: 32 (over x, z), mp: 8 (over y, core).
Axes of the slice: x: 4, y: 4, z: 8, core: 2. Of those that a mesh axis runs over, the one named last changes fastest.
Arguments:
- db_states: bfloat16 [96, 128, 8192], P('dp', 'mp'), may hold values from -6 to 6
- w_key: bfloat16 [8192, 4096], P('dp', 'mp'), may hold values from -0.0625 to 0.0625
- w_value: bfloat16 [8192, 4096], P('dp', 'mp'), may hold values from -0.0625 to 0.0625
- queries: bfloat16 [65536, 4096], P('dp', 'mp'), as said below
- nbr_owner: int32 [1024, 2], P('dp'), may hold values from 0 to 31, all different within a row; in each aligned block of 32 rows (0 to 31, 32 to 63, ...) at most 3 rows name the same one
- nbr_row: int32 [1024, 2], P('dp'), may hold values from 0 to 2
Outputs:
- attended: bfloat16 [65536, 4096], P('dp', 'mp')
Inputs may be any that keep to these rules, and one draw needn't show every extreme that they name: `nbr_owner`: among the 32 segments of one index of dp, at most 3 neighbours name the same owner; the two owners of one segment differ. `queries`: outside the shown draw query rows differ in scale by up to some eight times.
All inputs are finite; a program needn't handle non-finite values.
Results may differ from a plain program's by a relative error of at most 0.025.
Values may be sent and summed in bfloat16 or wider, within the bound.
No kernel may reach another device: no remote copies, remote signals or barrier semaphores. Data moves between devices by JAX's collectives and lax.ppermute only.
A program may use at most 192 MiB of HBM per device.

v0:
```python
import jax
import jax.numpy as jnp
from jax import lax
from jax.sharding import PartitionSpec as P

HDIM = 128
SEGMENT = 64


def local(db_states, w_key, w_value, queries, nbr_owner, nbr_row):
    groups = lax.axis_size("dp")
    columns = w_key.shape[1]
    heads_here = columns // HDIM
    held = db_states.shape[0]
    width = db_states.shape[2]
    seg_local = nbr_owner.shape[0]
    most_slots = max(2, 3 * seg_local // groups)
    key_full, value_full = (
        lax.all_gather(w_key, "dp", axis=0, tiled=True),
        lax.all_gather(w_value, "dp", axis=0, tiled=True),
    )
    rows_flat = lax.all_gather(db_states, "mp", axis=1, tiled=True).reshape(-1, width)
    key_part = jnp.dot(rows_flat, key_full, preferred_element_type=jnp.float32)
    value_part = jnp.dot(rows_flat, value_full, preferred_element_type=jnp.float32)
    encoded_pair = jnp.stack(
        [key_part.reshape(held, -1, columns), value_part.reshape(held, -1, columns)]
    )
    encoded = encoded_pair.astype(jnp.bfloat16)
    owner_ids = nbr_owner.reshape(-1)
    row_index = nbr_row.reshape(-1)
    listed = owner_ids.shape[0]
    position = jnp.arange(listed)
    same_owner = owner_ids[:, None] == owner_ids[None, :]
    earlier = position[None, :] < position[:, None]
    slot_rank = jnp.sum(jnp.logical_and(same_owner, earlier), axis=1)
    target = owner_ids * most_slots + slot_rank
    slots = groups * most_slots
    picked = jnp.arange(slots)[:, None] == target[None, :]
    segment_rows = queries.reshape(-1, SEGMENT * columns)
    per_neighbour = jnp.repeat(segment_rows, nbr_owner.shape[1], axis=0)
    send_queries = jnp.dot(
        picked.astype(jnp.bfloat16), per_neighbour, preferred_element_type=jnp.float32
    )
    send_queries = send_queries.astype(jnp.bfloat16).reshape(groups, most_slots, SEGMENT, columns)
    send_rows = jnp.sum(jnp.where(picked, row_index[None, :], 0), axis=1).reshape(
        groups, most_slots
    )
    scaling = HDIM ** (-0.5)
    query_in = lax.all_to_all(send_queries, "dp", split_axis=0, concat_axis=0, tiled=True)
    rows_in = lax.all_to_all(send_rows, "dp", split_axis=0, concat_axis=0, tiled=True)
    senders = query_in.shape[0]
    count = query_in.shape[1]
    which = (rows_in[..., None] == jnp.arange(held)[None, None, :]).astype(jnp.bfloat16)
    selected = jnp.einsum(
        "snb,ebtc->esntc", which, encoded, preferred_element_type=jnp.float32
    ).astype(jnp.bfloat16)
    query_heads = query_in.reshape(senders, count, SEGMENT, heads_here, HDIM)
    key_heads = selected[0].reshape(senders, count, -1, heads_here, HDIM)
    value_heads = selected[1].reshape(senders, count, -1, heads_here, HDIM)
    score = (
        jnp.einsum("snqhd,snkhd->snhqk", query_heads, key_heads, preferred_element_type=jnp.float32)
        * scaling
    )
    maxima = jnp.max(score, axis=-1)
    weights = jnp.exp(score - maxima[..., None])
    totals = jnp.sum(weights, axis=-1)
    partial_out = jnp.einsum("snhqk,snkhd->snqhd", weights, value_heads.astype(jnp.float32))
    partial_out = partial_out.reshape(senders, count, SEGMENT, columns).astype(jnp.bfloat16)
    returned, maxima, totals = (
        lax.all_to_all(partial_out, "dp", split_axis=0, concat_axis=0, tiled=True),
        lax.all_to_all(
            maxima.astype(jnp.bfloat16), "dp", split_axis=0, concat_axis=0, tiled=True
        ).astype(maxima.dtype),
        lax.all_to_all(
            totals.astype(jnp.bfloat16), "dp", split_axis=0, concat_axis=0, tiled=True
        ).astype(totals.dtype),
    )
    mine = returned.reshape(slots, SEGMENT, columns)[target]
    mine_max = maxima.reshape(slots, heads_here, SEGMENT)[target]
    mine_total = totals.reshape(slots, heads_here, SEGMENT)[target]
    pairs = nbr_owner.shape[1]
    mine = mine.reshape(-1, pairs, SEGMENT, heads_here, HDIM).astype(jnp.float32)
    mine_max = mine_max.reshape(-1, pairs, heads_here, SEGMENT)
    mine_total = mine_total.reshape(-1, pairs, heads_here, SEGMENT)
    highest = jnp.max(mine_max, axis=1)
    factor = jnp.exp(mine_max - highest[:, None])
    numer = jnp.sum(mine * jnp.transpose(factor, (0, 1, 3, 2))[..., None], axis=1)
    denom = jnp.sum(mine_total * factor, axis=1)
    output = numer / jnp.transpose(denom, (0, 2, 1))[..., None]
    return output.reshape(-1, columns).astype(jnp.bfloat16)


def solution(mesh):
    in_specs = (
        P("dp", "mp", None),
        P("dp", "mp"),
        P("dp", "mp"),
        P("dp", "mp"),
        P("dp", None),
        P("dp", None),
    )
    out_specs = P("dp", "mp")
    return jax.shard_map(local, mesh=mesh, in_specs=in_specs, out_specs=out_specs, check_vma=False)
```

profile of v0, /device:TPU:24, one launch (start us, length us, event | category | flops | bytes accessed | tf_op | source)
XLA Modules:
  0.0 671.0 jit_solution(15126106334257600904)
XLA Ops:
  6.5 0.7 all-gather.4.cloned.1.call-update
  7.3 0.7 all-gather.8.cloned.1.call-update
  8.1 0.7 all-gather.6.cloned.1.call-update
  8.7 0.8 copy.37
  9.5 0.1 reshape.108
  9.6 0.8 copy.38
  10.4 0.1 broadcast_in_dim.16
  10.5 0.2 convert_reduce_fusion
  10.7 0.1 select_reduce_fusion
  10.8 0.7 all_to_all.18
  11.5 11.3 %all-to-all-start = ((s32[32,1,3]{2,1,0:T(1,128)}), s32[32,1,3]{2,1,0:T(1,128)S(1)}, u32[]{:S(2)}, u32[]{:S(2)}) async-start(s32[32,1,3]{2,1,0:T(1,128)} %bitcast.5), calls=%async_computation | async-start | bytes 32768 | tf_op jit(solution)/shard_map/all_to_all | solution.py:50
  22.8 2.9 reshape.109
  25.8 3.6 broadcast_in_dim.19
  29.4 7.3 %reshape.110 = bf16[64,32768]{1,0:T(8,128)(2,1)} reshape(bf16[32,2,32768]{2,1,0:T(2,128)(2,1)} %broadcast_in_dim.19) | data formatting | bytes 8388608 | tf_op jit(solution)/shard_map/reshape | solution.py:40
  36.7 4.1 convolution_convert_fusion
  40.8 5.1 copy.55
  45.9 10.1 %all-to-all-start.1 = ((bf16[32,3,64,512]{3,2,1,0:T(8,128)(2,1)}), bf16[32,3,64,512]{3,2,1,0:T(8,128)(2,1)}, u32[]{:S(2)}, u32[]{:S(2)}) async-start(bf16[32,3,64,512]{3,2,1,0:T(8,128)(2,1)} %bitcast.91), calls=%async_computation.1 | async-start | bytes 12582912 | tf_op jit(solution)/shard_map/all_to_all | solution.py:49
  56.1 187.2 %all-gather.8.cloned.1.call-done = bf16[8192,512]{1,0:T(8,128)(2,1)} async-done(((bf16[256,512]{1,0:T(8,128)(2,1)}), bf16[8192,512]{1,0:T(8,128)(2,1)}) %all-gather.8.cloned.1.call-update) | async-done | bytes 8388624 | tf_op jit(solution)/shard_map/all_gather | solution.py:20
  243.3 8.6 %fusion.21 = bf16[1,3,128,512]{3,2,1,0:T(8,128)(2,1)S(1)} fusion(bf16[3,128,8192]{2,1,0:T(8,128)(2,1)} %all-gather.4.cloned.1.call-done, bf16[8192,512]{1,0:T(8,128)(2,1)} %all-gather.8.cloned.1.call-done), kind=kOutput, calls=%fused_computation.27 | convolution fusion | flops 3221422080 | bytes 15073280 | tf_op jit(solution)/shard_map/dot_general | solution.py:24
  251.9 91.3 %all-gather.6.cloned.1.call-done = bf16[8192,512]{1,0:T(8,128)(2,1)} async-done(((bf16[256,512]{1,0:T(8,128)(2,1)}), bf16[8192,512]{1,0:T(8,128)(2,1)}) %all-gather.6.cloned.1.call-update) | async-done | bytes 8388624 | tf_op jit(solution)/shard_map/all_gather | solution.py:19
  343.3 8.6 %fusion.24 = bf16[1,3,128,512]{3,2,1,0:T(8,128)(2,1)S(1)} fusion(bf16[3,128,8192]{2,1,0:T(8,128)(2,1)} %all-gather.4.cloned.1.call-done, bf16[8192,512]{1,0:T(8,128)(2,1)} %all-gather.6.cloned.1.call-done), kind=kOutput, calls=%fused_computation.28 | convolution fusion | flops 3221422080 | bytes 15073280 | tf_op jit(solution)/shard_map/dot_general | solution.py:23
  352.0 11.8 %convert_bitcast_fusion = bf16[2,32,3,128,512]{4,1,2,3,0:T(8,128)(2,1)} fusion(bf16[2,3,128,512,1]{3,2,1,0,4:T(8,128)(2,1)S(1)} %maximum_bitcast_fusion, s32[32,3]{0,1:T(4,128)S(1)} %bitcast.95), kind=kOutput, calls=%fused_computation.4 | convolution fusion | flops 88080672 | bytes 25952640 | tf_op jit(solution)/shard_map/snb,ebtc->esntc/dot_general | solution.py:54
  363.7 18.0 %fusion.37 = (bf16[1,32,3,128,512]{4,1,2,3,0:T(8,128)(2,1)}, bf16[1,32,3,128,512]{4,1,2,3,0:T(8,128)(2,1)}) fusion(bf16[2,32,3,128,512]{4,1,2,3,0:T(8,128)(2,1)} %convert_bitcast_fusion), kind=kLoop, calls=%fused_computation.54 | loop fusion | bytes 50331648 | tf_op jit(solution)/shard_map/slice | solution.py:59
  381.7 18.1 %reshape_squeeze.7 = bf16[32,3,128,4,128]{4,3,0,1,2:T(4,128)(2,1)} reshape(bf16[1,32,3,128,512]{4,1,2,3,0:T(8,128)(2,1)} %get-tuple-element.6) | data formatting | bytes 25165824 | tf_op jit(solution)/shard_map/reshape;squeeze | solution.py:58
  399.8 21.7 %multiply_reduce_fusion = (f32[32,3,4,64]{3,2,1,0:T(4,128)S(1)}, f32[32,3,4,64,128]{4,3,2,1,0:T(8,128)}) fusion(bf16[32,3,128,4,128]{4,3,0,1,2:T(4,128)(2,1)} %reshape_squeeze.7, bf16[32,3,64,512]{3,2,1,0:T(8,128)(2,1)} %all-to-all-done.1), kind=kOutput, calls=%fused_computation.10 | convolution fusion | flops 811573248 | bytes 31555584 | tf_op jit(solution)/shard_map/snqhd,snkhd->snhqk/dot_general | solution.py:61
  421.6 9.8 %fusion.4 = bf16[32,3,4,64]{3,2,1,0:T(4,128)(2,1)S(1)} fusion(f32[32,3,4,64,128]{4,3,2,1,0:T(8,128)} %get-tuple-element.10, f32[32,3,4,64]{3,2,1,0:T(4,128)S(1)} %get-tuple-element.9), kind=kLoop, calls=%fused_computation.11 | loop fusion | flops 9412608 | bytes 12730368 | tf_op jit(solution)/shard_map/reduce_sum | solution.py:66
  431.4 0.8 reshape.155
  432.2 5.6 all-to-all-start.4
  437.8 0.8 reshape.153
  438.6 18.1 %reshape_squeeze.6 = bf16[32,3,128,4,128]{4,3,0,1,2:T(4,128)(2,1)} reshape(bf16[1,32,3,128,512]{4,1,2,3,0:T(8,128)(2,1)} %get-tuple-element.5) | data formatting | bytes 25165824 | tf_op jit(solution)/shard_map/reshape;squeeze | solution.py:59
  456.8 10.0 %all-to-all-start.3 = ((bf16[32,2,384]{2,1,0:T(2,128)(2,1)}), bf16[32,2,384]{2,1,0:T(2,128)(2,1)S(1)}, u32[]{:S(2)}, u32[]{:S(2)}) async-start(bf16[32,2,384]{2,1,0:T(2,128)(2,1)} %reshape.153), calls=%async_computation.3 | async-start | bytes 98304 | tf_op jit(solution)/shard_map/all_to_all | solution.py:71
  466.8 18.6 %convert_bitcast_fusion.1 = bf16[32,3,4,8,8,128]{5,4,3,2,1,0:T(8,128)(2,1)S(1)} fusion(f32[32,3,4,64,128]{4,3,2,1,0:T(8,128)} %get-tuple-element.10, f32[32,3,4,64]{3,2,1,0:T(4,128)S(1)} %get-tuple-element.9, bf16[32,3,128,4,128]{4,3,0,1,2:T(4,128)(2,1)} %reshape_squeeze.6), kind=kOutput, calls=%fused_computation.20 | convolution fusion | flops 814743552 | bytes 31555584 | tf_op jit(solution)/shard_map/snhqk,snkhd->snqhd/dot_general | solution.py:67
  485.4 3.9 copy.75
  489.3 9.8 %all-to-all-start.2 = ((bf16[32,3,64,512]{3,2,1,0:T(8,128)(2,1)}), bf16[32,3,64,512]{3,2,1,0:T(8,128)(2,1)}, u32[]{:S(2)}, u32[]{:S(2)}) async-start(bf16[32,3,64,512]{3,2,1,0:T(8,128)(2,1)} %bitcast.90), calls=%async_computation.2 | async-start | bytes 12582912 | tf_op jit(solution)/shard_map/all_to_all | solution.py:70
  499.1 0.1 copy.46
  499.2 0.1 mul.47
  499.3 0.1 reshape.156
  499.5 0.7 gather_fusion.2
  500.1 0.1 reshape.154
  500.3 0.7 gather_fusion.1
  501.1 0.7 copy.47
  501.8 0.4 copy.48
  502.2 134.7 %all-to-all-done.2 = bf16[32,3,64,512]{3,2,1,0:T(8,128)(2,1)} async-done(((bf16[32,3,64,512]{3,2,1,0:T(8,128)(2,1)}), bf16[32,3,64,512]{3,2,1,0:T(8,128)(2,1)}, u32[]{:S(2)}, u32[]{:S(2)}) %all-to-all-start.2) | async-done | bytes 6291488 | tf_op jit(solution)/shard_map/all_to_all | solution.py:70
  636.9 5.6 gather_fusion
  642.5 8.3 %reshape.120 = f32[32,2,64,4,128]{4,3,2,1,0:T(4,128)} reshape(bf16[64,64,512]{2,1,0:T(8,128)(2,1)} %gather_fusion) | data formatting | bytes 12582912 | tf_op jit(solution)/shard_map/convert_element_type | solution.py:82
  650.8 9.5 %multiply_reduce_fusion.1 = f32[32,64,4,128]{3,2,1,0:T(4,128)S(1)} fusion(f32[32,2,64,4,128]{4,3,2,1,0:T(4,128)} %reshape.120, f32[32,2,64,4]{3,2,1,0:T(8,128)S(1)} %copy.47), kind=kLoop, calls=%fused_computation.16 | loop fusion | flops 3145728 | bytes 12648448 | tf_op jit(solution)/shard_map/reduce_sum | solution.py:87
  660.2 2.5 divide_convert_fusion
  662.8 1.7 copy.76
  (21 shorter events, 0.5 us)
Async XLA Ops:
  6.5 49.6 %all-gather.4.cloned.1.call-start = ((), (), s32[]{:S(2)}) async-start(), calls=%async_computation.5 | async-start | bytes 7077888 | tf_op jit(solution)/shard_map/all_gather | solution.py:22
  7.3 236.1 %all-gather.8.cloned.1.call-start = ((), (), s32[]{:S(2)}) async-start(), calls=%async_computation.7 | async-start | bytes 8650752 | tf_op jit(solution)/shard_map/all_gather | solution.py:20
  8.0 335.3 %all-gather.6.cloned.1.call-start = ((), (), s32[]{:S(2)}) async-start(), calls=%async_computation.6 | async-start | bytes 8650752 | tf_op jit(solution)/shard_map/all_gather | solution.py:19
  11.5 34.4 %all-to-all-start = ((s32[32,1,3]{2,1,0:T(1,128)}), s32[32,1,3]{2,1,0:T(1,128)S(1)}, u32[]{:S(2)}, u32[]{:S(2)}) async-start(s32[32,1,3]{2,1,0:T(1,128)} %bitcast.5), calls=%async_computation | async-start | bytes 32768 | tf_op jit(solution)/shard_map/all_to_all | solution.py:50
  45.9 353.9 %all-to-all-start.1 = ((bf16[32,3,64,512]{3,2,1,0:T(8,128)(2,1)}), bf16[32,3,64,512]{3,2,1,0:T(8,128)(2,1)}, u32[]{:S(2)}, u32[]{:S(2)}) async-start(bf16[32,3,64,512]{3,2,1,0:T(8,128)(2,1)} %bitcast.91), calls=%async_computation.1 | async-start | bytes 12582912 | tf_op jit(solution)/shard_map/all_to_all | solution.py:49
  432.2 24.6 %all-to-all-start.4 = ((bf16[32,2,384]{2,1,0:T(2,128)(2,1)}), bf16[32,2,384]{2,1,0:T(2,128)(2,1)S(1)}, u32[]{:S(2)}, u32[]{:S(2)}) async-start(bf16[32,2,384]{2,1,0:T(2,128)(2,1)} %reshape.155), calls=%async_computation.4 | async-start | bytes 98304 | tf_op jit(solution)/shard_map/all_to_all | solution.py:74
  456.8 32.5 %all-to-all-start.3 = ((bf16[32,2,384]{2,1,0:T(2,128)(2,1)}), bf16[32,2,384]{2,1,0:T(2,128)(2,1)S(1)}, u32[]{:S(2)}, u32[]{:S(2)}) async-start(bf16[32,2,384]{2,1,0:T(2,128)(2,1)} %reshape.153), calls=%async_computation.3 | async-start | bytes 98304 | tf_op jit(solution)/shard_map/all_to_all | solution.py:71
  489.3 9.8 %copy-start = (s32[32,2]{0,1:T(2,128)S(1)}, s32[32,2]{0,1:T(2,128)}, u32[]{:S(2)}) copy-start(s32[32,2]{0,1:T(2,128)} %param.10) | copy-start | bytes 772
  489.3 147.7 %all-to-all-start.2 = ((bf16[32,3,64,512]{3,2,1,0:T(8,128)(2,1)}), bf16[32,3,64,512]{3,2,1,0:T(8,128)(2,1)}, u32[]{:S(2)}, u32[]{:S(2)}) async-start(bf16[32,3,64,512]{3,2,1,0:T(8,128)(2,1)} %bitcast.90), calls=%async_computation.2 | async-start | bytes 12582912 | tf_op jit(solution)/shard_map/all_to_all | solution.py:70
Sparse Core Ops, SparseCore 0:
  9.2 44.2 all-gather.3
  56.1 187.2 all-gather.7
  245.9 97.3 all-gather.5
where the time goes:
time: 674 us; the launch traced here: 671 us
  waiting for transfers between devices  415 us (62%)
  local copies, waits for them, and re-layouts  99.5 us (15%)
  matrix products  73.4 us (11%)
  starting transfers between devices  46.9 us (7%)
  other arithmetic  22.3 us (3%)
  between operations  13.3 us (2%)
    all_gather x1, waiting for transfers between devices, local(): lax.all_gather(w_value, 'dp', axis=0, tiled=True)  187 us
    all_to_all x1, waiting for transfers between devices, local(): lax.all_to_all(partial_out, 'dp', split_axis=0, concat_axis=0, tiled=True)  135 us
    all_gather x1, waiting for transfers between devices, local(): lax.all_gather(w_key, 'dp', axis=0, tiled=True)  91.3 us
    dot_general x1, matrix products, local(): jnp.einsum('snqhd,snkhd->snhqk', query_heads, key_heads, preferred_elemen...  21.7 us
    dot_general x1, matrix products, local(): jnp.einsum('snhqk,snkhd->snqhd', weights, value_heads.astype(jnp.float32))  18.6 us
    another operation x1, local copies, waits for them, and re-layouts, local(): key_heads = selected[0].reshape(senders, count, -1, heads_here, HDIM)  18.1 us
    another operation x1, local copies, waits for them, and re-layouts, local(): value_heads = selected[1].reshape(senders, count, -1, heads_here, HDIM)  18.1 us
    slice x1, local copies, waits for them, and re-layouts, local(): value_heads = selected[1].reshape(senders, count, -1, heads_here, HDIM)  18 us
  transfers between devices with their start and end apart: 8, of which 3 were waited for; matrix products, arithmetic and copies ran while one was open for 20% of the time, Pallas kernels for 0%

commit v1 on v0

v1 whole, which is shorter than its diff:
```python
import functools

import jax
import jax.numpy as jnp
from jax import lax
from jax.experimental import pallas as pl
from jax.experimental.pallas import tpu as pltpu
from jax.sharding import PartitionSpec as P

HDIM = 128
SEGMENT = 64
XN, ZN = 4, 8
HELD = 3
TOK = 64
CHUNK_HEADS = 2
BF = jnp.bfloat16
F32 = jnp.float32


def moved(array, to):
    pairs = []
    for x in range(XN):
        for z in range(ZN):
            tx, tz = to(x, z)
            pairs.append((x * ZN + z, (tx % XN) * ZN + tz % ZN))
    return lax.ppermute(array, "dp", pairs)


def up(array):
    return moved(array, lambda x, z: (x, z + 1))


def down(array):
    return moved(array, lambda x, z: (x, z - 1))


def cross(array):
    return moved(array, lambda x, z: (x ^ 3, z))


def pair(array):
    return moved(array, lambda x, z: (x ^ 1, z))


def gather16(a, b):
    rows = a.shape[0]
    half = rows // 2
    join = functools.partial(jnp.concatenate, axis=0)
    up1, down1, other_a = up(b), down(b), cross(a)
    up2 = up(join([a, other_a, up1]))
    down2 = down(join([other_a, a, down1]))
    side2 = cross(join([b, up1, down1]))
    up3, down3 = up(up2), down(down2)
    side3 = cross(join([up2[2 * rows :], down2[2 * rows :]]))
    up4 = up(up3[: 2 * rows + half])
    down4 = down(join([down3[: 2 * rows], down3[2 * rows + half :]]))
    side4 = cross(join([up3[2 * rows :], down3[2 * rows :]]))
    up5, down5 = up(up4[:rows]), down(down4[:rows])
    side5 = cross(join([up4[2 * rows :], down4[2 * rows :]]))
    arrays = [a, b, other_a, up1, down1, up2, down2, side2, up3, down3, side3, up4, down4, side4, up5, down5, side5]
    pieces = [
        (0, 0, rows, 0, 0, 0),
        (1, 0, rows, 1, 0, 0),
        (2, 0, rows, 0, 8, 0),
        (3, 0, rows, 1, 1, 0),
        (4, 0, rows, 1, 7, 0),
        (7, 0, rows, 1, 8, 0),
        (7, rows, rows, 1, 9, 0),
        (7, 2 * rows, rows, 1, 15, 0),
        (10, 0, rows, 1, 10, 0),
        (10, rows, rows, 1, 14, 0),
        (13, 0, rows, 1, 11, 0),
        (13, rows, rows, 1, 13, 0),
        (14, 0, rows, 0, 4, 0),
        (15, 0, rows, 0, 12, 0),
        (16, 0, rows, 1, 12, 0),
        (11, 2 * rows, half, 1, 4, 0),
        (12, 2 * rows, half, 1, 4, half),
        (5, 2 * rows, rows, 1, 2, 0),
        (6, 2 * rows, rows, 1, 6, 0),
        (8, 2 * rows, rows, 1, 3, 0),
        (9, 2 * rows, rows, 1, 5, 0),
    ]
    for step, array in ((1, 5), (2, 8), (3, 11)):
        pieces += [(array, 0, rows, 0, step, 0), (array, rows, rows, 0, 8 + step, 0)]
    for step, array in ((1, 6), (2, 9), (3, 12)):
        pieces += [(array, 0, rows, 0, 16 - step, 0), (array, rows, rows, 0, 8 - step, 0)]
    return arrays, pieces


ROW_TILE = 192


def project_kernel(pieces, place_ref, half_ref, db_hbm, *refs):
    count = 17
    w_refs = refs[:count]
    mine_k, mine_v, send_k, send_v, db_ref, w_ref, db_sem, w_sem = refs[count:]
    db_copy = pltpu.make_async_copy(db_hbm, db_ref, db_sem)
    db_copy.start()
    copies = []
    for i, (array, first, rows, kind, place, at) in enumerate(pieces):
        copies.append(
            pltpu.make_async_copy(
                w_refs[array].at[pl.ds(first, rows)],
                w_ref.at[kind, place_ref[place], pl.ds(at, rows)],
                w_sem.at[i],
            )
        )
        copies[-1].start()
    db_copy.wait()
    for copy in copies:
        copy.wait()
    depth = w_ref.shape[1] * w_ref.shape[2]
    width = w_ref.shape[3]
    blocks = db_ref.shape[0] // 2 // 16
    per_tile = ROW_TILE // 16
    entries = 2 * HELD
    for own in (0, 1):
        side = half_ref[0] if own else 1 - half_ref[0]
        for tile in range(blocks // per_tile):
            start = pl.multiple_of(side * (blocks * 16) + tile * ROW_TILE, ROW_TILE)
            rows = db_ref[pl.ds(start, ROW_TILE), :]
            for kind in (0, 1):
                part = jnp.dot(rows, w_ref[kind].reshape(depth, width), preferred_element_type=F32)
                for j in range(per_tile):
                    group, entry = divmod(tile * per_tile + j, entries)
                    target = entry * TOK + group * 16
                    piece = part[j * 16 : (j + 1) * 16]
                    if own:
                        (mine_v if kind else mine_k)[target : target + 16, :] = piece
                    else:
                        (send_v if kind else send_k)[target : target + 16, :] = piece.astype(BF)


def project(db, arrays, pieces, places, side):
    rows, depth = db.shape
    width = arrays[0].shape[1]
    half = rows // 2
    vmem = pl.BlockSpec(memory_space=pltpu.VMEM)
    anywhere = pl.BlockSpec(memory_space=pl.ANY)
    smem = pl.BlockSpec(memory_space=pltpu.SMEM)
    return pl.pallas_call(
        functools.partial(project_kernel, pieces),
        out_shape=[jax.ShapeDtypeStruct((half, width), F32)] * 2 + [jax.ShapeDtypeStruct((half, width), BF)] * 2,
        in_specs=[smem, smem] + [anywhere] * (1 + len(arrays)),
        out_specs=[vmem] * 4,
        scratch_shapes=[
            pltpu.VMEM((rows, depth), BF),
            pltpu.VMEM((2, 16, depth // 16, width), BF),
            pltpu.SemaphoreType.DMA,
            pltpu.SemaphoreType.DMA((len(pieces),)),
        ],
        compiler_params=pltpu.CompilerParams(vmem_limit_bytes=48 << 20),
        cost_estimate=pl.CostEstimate(flops=4 * rows * depth * width, bytes_accessed=24 << 20, transcendentals=0),
        name="project",
    )(places, side, db, *arrays)


def attend_kernel(pieces, first_head, slot_ref, q_ref, *refs):
    count = 17
    kv_refs = refs[:count]
    out_ref, stat_ref, kv_ref, sem = refs[count:]
    copies = []
    for i, (array, first, rows, kind, place, at) in enumerate(pieces):
        copies.append(
            pltpu.make_async_copy(
                kv_refs[array].at[pl.ds(first, rows)],
                kv_ref.at[kind, pl.ds(place * 6 * TOK + at, rows)],
                sem.at[i],
            )
        )
        copies[-1].start()
    for copy in copies:
        copy.wait()
    stat_ref[...] = jnp.zeros_like(stat_ref)
    lane = lax.broadcasted_iota(jnp.int32, (SEGMENT, 128), 1)
    heads = q_ref.shape[1] // HDIM

    def unit(u, carry):
        at = pl.multiple_of(u * SEGMENT, SEGMENT)
        one = pl.multiple_of(slot_ref[2 * u] * TOK, TOK)
        two = pl.multiple_of(slot_ref[2 * u + 1] * TOK, TOK)
        stat = stat_ref[...]
        for j in range(heads):
            cols = slice(j * HDIM, (j + 1) * HDIM)
            q = q_ref[pl.ds(at, SEGMENT), cols]
            keys = jnp.concatenate([kv_ref[0, pl.ds(one, TOK), cols], kv_ref[0, pl.ds(two, TOK), cols]], axis=0)
            values = jnp.concatenate([kv_ref[1, pl.ds(one, TOK), cols], kv_ref[1, pl.ds(two, TOK), cols]], axis=0)
            score = lax.dot_general(q, keys, (((1,), (1,)), ((), ())), preferred_element_type=F32) * (HDIM**-0.5)
            top = jnp.max(score, axis=1, keepdims=True)
            weight = jnp.exp(score - top)
            total = jnp.sum(weight, axis=1, keepdims=True)
            mixed = jnp.dot(weight.astype(BF), values, preferred_element_type=F32)
            out_ref[pl.ds(at, SEGMENT), cols] = (mixed / total).astype(BF)
            stat = jnp.where(lane == u * heads + j, top + jnp.log(total), stat)
        stat_ref[...] = stat
        return carry

    lax.fori_loop(0, q_ref.shape[0] // SEGMENT, unit, 0, unroll=4)


def attend(slots, queries, chunk, arrays, pieces):
    rows = queries.shape[0]
    width = arrays[0].shape[1]
    block = arrays[0].shape[0]
    smem = pl.BlockSpec(memory_space=pltpu.SMEM)
    anywhere = pl.BlockSpec(memory_space=pl.ANY)
    return pl.pallas_call(
        functools.partial(attend_kernel, pieces, chunk * CHUNK_HEADS),
        grid=(1,),
        out_shape=[jax.ShapeDtypeStruct((rows, width), BF), jax.ShapeDtypeStruct((SEGMENT, 128), F32)],
        in_specs=[smem, pl.BlockSpec((rows, width), lambda i: (0, chunk))] + [anywhere] * len(arrays),
        out_specs=[pl.BlockSpec((rows, width), lambda i: (0, 0)), pl.BlockSpec((SEGMENT, 128), lambda i: (0, 0))],
        scratch_shapes=[pltpu.VMEM((2, 16 * block, width), BF), pltpu.SemaphoreType.DMA((len(pieces),))],
        compiler_params=pltpu.CompilerParams(vmem_limit_bytes=40 << 20),
        cost_estimate=pl.CostEstimate(flops=4 * rows * 128 * width, bytes_accessed=10 << 20, transcendentals=rows * width),
        name="attend",
    )(slots, queries, *arrays)


def merge_kernel(mine_ref, theirs_ref, stat_ref, other_ref, *refs):
    out_ref = refs[-1]
    lane = lax.broadcasted_iota(jnp.int32, (SEGMENT, 128), 1)
    heads = mine_ref.shape[1] // HDIM
    difference = other_ref[...] - stat_ref[...]

    def unit(u, carry):
        at = pl.multiple_of(u * SEGMENT, SEGMENT)
        for j in range(heads):
            cols = slice(j * HDIM, (j + 1) * HDIM)
            gap = jnp.sum(jnp.where(lane == u * heads + j, difference, 0.0), axis=1, keepdims=True)
            small = jnp.exp(-jnp.abs(gap))
            larger = 1.0 / (1.0 + small)
            smaller = small * larger
            share = jnp.where(gap > 0, smaller, larger)
            rest = jnp.where(gap > 0, larger, smaller)
            a = mine_ref[pl.ds(at, SEGMENT), cols].astype(F32)
            b = theirs_ref[pl.ds(at, SEGMENT), cols].astype(F32)
            out_ref[pl.ds(at, SEGMENT), cols] = (a * share + b * rest).astype(BF)
        return carry

    lax.fori_loop(0, mine_ref.shape[0] // SEGMENT, unit, 0, unroll=4)


def merge(mine, theirs, stat, other, chunk, full_width, so_far):
    rows, width = mine.shape
    whole = pl.BlockSpec((rows, width), lambda i: (0, 0))
    stats = pl.BlockSpec((SEGMENT, 128), lambda i: (0, 0))
    extra = [] if so_far is None else [so_far]
    return pl.pallas_call(
        merge_kernel,
        grid=(1,),
        out_shape=jax.ShapeDtypeStruct((rows, full_width), BF),
        in_specs=[whole, whole, stats, stats] + [pl.BlockSpec(memory_space=pl.ANY)] * len(extra),
        out_specs=pl.BlockSpec((rows, width), lambda i: (0, chunk)),
        input_output_aliases={4: 0} if extra else {},
        compiler_params=pltpu.CompilerParams(vmem_limit_bytes=32 << 20),
        cost_estimate=pl.CostEstimate(flops=8 * rows * width, bytes_accessed=6 * rows * width, transcendentals=rows),
        name="merge",
    )(mine, theirs, stat, other, *extra)


def local(db_states, w_key, w_value, queries, nbr_owner, nbr_row):
    place = lax.axis_index("dp")
    x, z = place // ZN, place % ZN
    side = ((x + 1) // 2) % 2
    quarter = db_states.shape[2] // XN

    outer = jnp.concatenate([db_states[..., :quarter], db_states[..., 3 * quarter :]], axis=-1)
    inner = db_states[..., quarter : 3 * quarter]
    kept = jnp.where(side == 0, outer, inner)
    given = pair(jnp.where(side == 0, inner, outer))
    even = x % 2 == 0
    six = jnp.concatenate([jnp.where(even, kept, given), jnp.where(even, given, kept)], axis=0)
    db = lax.all_gather(six, "mp", axis=0, tiled=False).reshape(-1, 2 * quarter)

    w_arrays, w_pieces = gather16(w_key, w_value)
    their_queries = pair(queries)
    tables = pair(jnp.concatenate([nbr_owner, nbr_row], axis=1))

    k = jnp.arange(ZN)
    near = (z - k) % ZN + jnp.where(x >= 2, ZN, 0)
    far = (z - k) % ZN + jnp.where(x >= 2, 0, ZN)
    places = jnp.concatenate([near, far]).astype(jnp.int32)
    mine_k, mine_v, send_k, send_v = project(db, w_arrays, w_pieces, places, side.reshape(1).astype(jnp.int32))

    def slots(owner, row):
        from_x, from_z = owner // ZN, owner % ZN
        block = jnp.where(from_x // 2 == x // 2, 0, ZN) + (z - from_z) % ZN
        return (block * (2 * HELD) + (from_x % 2) * HELD + row).reshape(-1).astype(jnp.int32)

    own_slots = slots(nbr_owner, nbr_row)
    their_slots = slots(tables[:, :2], tables[:, 2:])

    width = CHUNK_HEADS * HDIM
    columns = queries.shape[1]
    output = None
    for chunk in range(columns // width):
        cols = slice(chunk * width, (chunk + 1) * width)
        got = pair(jnp.concatenate([send_k[:, cols], send_v[:, cols]], axis=0))
        half = got.shape[0] // 2
        keys = (mine_k[:, cols] + got[:half].astype(F32)).astype(BF)
        values = (mine_v[:, cols] + got[half:].astype(F32)).astype(BF)
        arrays, pieces = gather16(keys, values)
        given, given_stat = attend(their_slots, their_queries, chunk, arrays, pieces)
        theirs, other = pair(given), pair(given_stat)
        mine, stat = attend(own_slots, queries, chunk, arrays, pieces)
        output = merge(mine, theirs, stat, other, chunk, columns, output)
    return output


def solution(mesh):
    in_specs = (
        P("dp", "mp", None),
        P("dp", "mp"),
        P("dp", "mp"),
        P("dp", "mp"),
        P("dp", None),
        P("dp", None),
    )
    out_specs = P("dp", "mp")
    return jax.shard_map(local, mesh=mesh, in_specs=in_specs, out_specs=out_specs, check_vma=False)
```

time: 674 us -> 409 us (0.61)
  waiting for transfers between devices: 415 us -> 129 us
  Pallas kernels: 0 us -> 119 us
  matrix products: 73.4 us -> 0 us
  local copies, waits for them, and re-layouts: 99.5 us -> 40.3 us
  starting transfers between devices: 46.9 us -> 89.8 us
  other arithmetic: 22.3 us -> 8.61 us
    all_gather x3 -> x1, waiting for transfers between devices: 279 us -> 0.01 us  [local(): db = lax.all_gather(six, 'mp', axis=0, tiled=False).reshape(-1, 2 * quarter)]
    all_to_all x5 -> x0, waiting for transfers between devices: 135 us -> none  [the longest x1 135 us: local(): lax.all_to_all(partial_out, 'dp', split_axis=0, concat_axis=0, tiled=True)]
    ppermute x0 -> x54, waiting for transfers between devices: none -> 129 us  [moved(): return lax.ppermute(array, 'dp', pairs)]
    pallas_call x0 -> x7, Pallas kernels: none -> 119 us  [the longest x4 98 us: attend(): pl.pallas_call(functools.partial(attend_kernel, pieces, chunk * CHUNK_HEA...]
    ppermute x0 -> x54, starting transfers between devices: none -> 89.8 us  [moved(): return lax.ppermute(array, 'dp', pairs)]
    dot_general x6 -> x0, matrix products: 73.4 us -> none  [the longest x1 21.7 us: local(): jnp.einsum('snqhd,snkhd->snhqk', query_heads, key_heads, preferred_elemen...]
    all_to_all x5 -> x0, starting transfers between devices: 46.9 us -> none  [the longest x1 11.3 us: local(): lax.all_to_all(send_rows, 'dp', split_axis=0, concat_axis=0, tiled=True)]
    another operation x2 -> x0, local copies, waits for them, and re-layouts: 36.3 us -> none  [the longest x1 18.1 us: local(): key_heads = selected[0].reshape(senders, count, -1, heads_here, HDIM)]
  transfers between devices with their start and end apart: 8 -> 55, of which waited for: 3 -> 22; matrix products, arithmetic and copies ran while one was open for 20% -> 4% of each run, Pallas kernels for 0% -> 25%
where the time goes in v1:
time: 409 us; the launch traced here: 401 us
  waiting for transfers between devices  129 us (32%)
  Pallas kernels  119 us (29%)
  starting transfers between devices  89.8 us (22%)
  local copies, waits for them, and re-layouts  40.3 us (10%)
  between operations  14.7 us (4%)
  other arithmetic  8.61 us (2%)
    ppermute x54, waiting for transfers between devices, moved(): return lax.ppermute(array, 'dp', pairs)  129 us
    pallas_call x4, Pallas kernels, attend(): pl.pallas_call(functools.partial(attend_kernel, pieces, chunk * CHUNK_HEA...  98 us
    ppermute x54, starting transfers between devices, moved(): return lax.ppermute(array, 'dp', pairs)  89.8 us
    unnamed x176, local copies, waits for them, and re-layouts  30.9 us
    pallas_call x1, Pallas kernels, project(): pl.pallas_call(functools.partial(project_kernel, pieces), out_shape=[jax....  12.6 us
  transfers between devices with their start and end apart: 55, of which 22 were waited for; matrix products, arithmetic and copies ran while one was open for 4% of the time, Pallas kernels for 25%

profile of v1, /device:TPU:24, one launch (start us, length us, event | category | flops | bytes accessed | tf_op | source)
XLA Modules:
  0.0 400.7 jit_solution(13738925373607991211)
XLA Ops:
  10.3 9.4 %collective-permute-done = bf16[3,16,4096]{2,1,0:T(8,128)(2,1)S(1)} collective-permute-done((bf16[3,16,4096]{2,1,0:T(8,128)(2,1)S(1)}, bf16[3,16,4096]{2,1,0:T(8,128)(2,1)S(1)}, u32[]{:S(2)}, u32[]{:S(2)}) %collective-permute-start) | collective-permute-done | bytes 393248 | tf_op jit(solution)/shard_map/ppermute | solution.py:26
  20.9 2.8 collective-permute-start.1
  23.8 1.9 collective-permute-start.2
  25.7 3.9 collective-permute-start.3
  29.6 5.1 %collective-permute-done.2.refs_3_ = bf16[256,512]{1,0:T(8,128)(2,1)S(1)} collective-permute-done((bf16[256,512]{1,0:T(8,128)(2,1)S(1)}, bf16[256,512]{1,0:T(8,128)(2,1)S(1)}, u32[]{:S(2)}, u32[]{:S(2)}) %collective-permute-start.2) | collective-permute-done | bytes 262176 | tf_op jit(solution)/shard_map/ppermute | solution.py:26
  35.0 3.2 collective-permute-start.5
  38.3 15.5 %collective-permute-done.4.refs_5_ = bf16[768,512]{1,0:T(8,128)(2,1)S(1)} collective-permute-done((bf16[768,512]{1,0:T(8,128)(2,1)S(1)}, bf16[768,512]{1,0:T(8,128)(2,1)S(1)}, u32[]{:S(2)}, u32[]{:S(2)}) %collective-permute-start.4) | collective-permute-done | bytes 786464 | tf_op jit(solution)/shard_map/ppermute | solution.py:26
  53.8 3.2 collective-permute-start.8
  57.5 14.2 %collective-permute-done.7.refs_8_ = bf16[768,512]{1,0:T(8,128)(2,1)S(1)} collective-permute-done((bf16[768,512]{1,0:T(8,128)(2,1)S(1)}, bf16[768,512]{1,0:T(8,128)(2,1)S(1)}, u32[]{:S(2)}, u32[]{:S(2)}) %collective-permute-start.7) | collective-permute-done | bytes 786464 | tf_op jit(solution)/shard_map/ppermute | solution.py:26
  71.9 3.3 collective-permute-start.11
  77.4 2.8 collective-permute-start.12
  80.2 5.7 %collective-permute-done.10.refs_11_ = bf16[640,512]{1,0:T(8,128)(2,1)S(1)} collective-permute-done((bf16[640,512]{1,0:T(8,128)(2,1)S(1)}, bf16[640,512]{1,0:T(8,128)(2,1)S(1)}, u32[]{:S(2)}, u32[]{:S(2)}) %collective-permute-start.10) | collective-permute-done | bytes 655392 | tf_op jit(solution)/shard_map/ppermute | solution.py:26
  87.4 3.2 collective-permute-start.14
  93.0 8.2 %collective-permute-done.12.refs_13_ = bf16[512,512]{1,0:T(8,128)(2,1)} collective-permute-done((bf16[512,512]{1,0:T(8,128)(2,1)}, bf16[512,512]{1,0:T(8,128)(2,1)}, u32[]{:S(2)}, u32[]{:S(2)}) %collective-permute-start.12) | collective-permute-done | bytes 524320 | tf_op jit(solution)/shard_map/ppermute | solution.py:26
  101.2 2.8 collective-permute-done.15.refs_16_
  104.0 12.6 %project.1 = (f32[384,512]{1,0:T(8,128)S(1)}, f32[384,512]{1,0:T(8,128)}, bf16[384,512]{1,0:T(8,128)(2,1)S(1)}, bf16[384,512]{1,0:T(8,128)(2,1)S(1)}) custom-call(s32[16]{0:T(128)S(1)} %pad_add_fusion.1.place_ref, s32[1]{0:T(128)} %bitcast.half_ref, bf16[768,4096]{1,0:T(8,128)(2,1)} %bitcast.2, bf16[256,512]{1,0:T(8,128)(2,1)S(1)} %copy-done.77, ...), custom_call_target="tpu_custom_call" | custom-call | flops 6442450944 | bytes 25165824 | tf_op jit(solution)/shard_map/project/pallas_call | solution.py:142
  116.9 2.1 collective-permute-start.16
  119.0 7.9 %collective-permute-done.36 = bf16[768,256]{1,0:T(8,128)(2,1)S(1)} collective-permute-done((bf16[768,256]{1,0:T(8,128)(2,1)S(1)}, bf16[768,256]{1,0:T(8,128)(2,1)S(1)}, u32[]{:S(2)}, u32[]{:S(2)}) %collective-permute-start.36) | collective-permute-done | bytes 393248 | tf_op jit(solution)/shard_map/ppermute | solution.py:26
  126.9 4.4 %collective-permute-done.16 = bf16[768,256]{1,0:T(8,128)(2,1)S(1)} collective-permute-done((bf16[768,256]{1,0:T(8,128)(2,1)S(1)}, bf16[768,256]{1,0:T(8,128)(2,1)S(1)}, u32[]{:S(2)}, u32[]{:S(2)}) %collective-permute-start.16) | collective-permute-done | bytes 393248 | tf_op jit(solution)/shard_map/ppermute | solution.py:26
  132.0 3.2 collective-permute-start.39
  135.2 4.1 %collective-permute-done.37.refs_2_ = bf16[384,256]{1,0:T(8,128)(2,1)S(1)} collective-permute-done((bf16[384,256]{1,0:T(8,128)(2,1)S(1)}, bf16[384,256]{1,0:T(8,128)(2,1)S(1)}, u32[]{:S(2)}, u32[]{:S(2)}) %collective-permute-start.37) | collective-permute-done | bytes 196640 | tf_op jit(solution)/shard_map/ppermute | solution.py:26
  139.5 4.4 %collective-permute-start.17 = (bf16[384,256]{1,0:T(8,128)(2,1)S(1)}, bf16[384,256]{1,0:T(8,128)(2,1)S(1)}, u32[]{:S(2)}, u32[]{:S(2)}) collective-permute-start(bf16[384,256]{1,0:T(8,128)(2,1)S(1)} %get-tuple-element.34.refs_0_), channel_id=1, source_target_pairs={{0,192},{8,200},{16,208},{24,216},{32,224},{40,232},{48,240},{56,2... | collective-permute-start | bytes 589832 | tf_op jit(solution)/shard_map/ppermute | solution.py:26
  144.6 3.0 collective-permute-done.17.refs_2_
  147.5 9.0 %collective-permute-start.41 = (bf16[1152,256]{1,0:T(8,128)(2,1)S(1)}, bf16[1152,256]{1,0:T(8,128)(2,1)S(1)}, u32[]{:S(2)}, u32[]{:S(2)}) collective-permute-start(bf16[1152,256]{1,0:T(8,128)(2,1)S(1)} %get-tuple-element.42), channel_id=1, source_target_pairs={{0,56},{8,0},{16,8},{24,16},{32,24},{40,32},{48,40},{56,48},{64,12... | collective-permute-start | bytes 1769480 | tf_op jit(solution)/shard_map/ppermute | solution.py:26
  161.0 11.5 %collective-permute-done.41.refs_6_ = bf16[1152,256]{1,0:T(8,128)(2,1)S(1)} collective-permute-done((bf16[1152,256]{1,0:T(8,128)(2,1)S(1)}, bf16[1152,256]{1,0:T(8,128)(2,1)S(1)}, u32[]{:S(2)}, u32[]{:S(2)}) %collective-permute-start.41) | collective-permute-done | bytes 589856 | tf_op jit(solution)/shard_map/ppermute | solution.py:26
  175.2 9.9 %collective-permute-done.21.refs_6_ = bf16[1152,256]{1,0:T(8,128)(2,1)S(1)} collective-permute-done((bf16[1152,256]{1,0:T(8,128)(2,1)S(1)}, bf16[1152,256]{1,0:T(8,128)(2,1)S(1)}, u32[]{:S(2)}, u32[]{:S(2)}) %collective-permute-start.21) | collective-permute-done | bytes 589856 | tf_op jit(solution)/shard_map/ppermute | solution.py:26
  187.4 2.9 collective-permute-start.22
  190.3 7.4 %collective-permute-done.44.refs_9_ = bf16[1152,256]{1,0:T(8,128)(2,1)S(1)} collective-permute-done((bf16[1152,256]{1,0:T(8,128)(2,1)S(1)}, bf16[1152,256]{1,0:T(8,128)(2,1)S(1)}, u32[]{:S(2)}, u32[]{:S(2)}) %collective-permute-start.44) | collective-permute-done | bytes 589856 | tf_op jit(solution)/shard_map/ppermute | solution.py:26
  198.9 2.3 collective-permute-start.47
  201.2 5.3 %collective-permute-done.24.refs_9_ = bf16[1152,256]{1,0:T(8,128)(2,1)S(1)} collective-permute-done((bf16[1152,256]{1,0:T(8,128)(2,1)S(1)}, bf16[1152,256]{1,0:T(8,128)(2,1)S(1)}, u32[]{:S(2)}, u32[]{:S(2)}) %collective-permute-start.24) | collective-permute-done | bytes 589856 | tf_op jit(solution)/shard_map/ppermute | solution.py:26
  206.9 3.2 collective-permute-done.32
  210.1 4.3 %collective-permute-start.42 = (bf16[1152,256]{1,0:T(8,128)(2,1)S(1)}, bf16[1152,256]{1,0:T(8,128)(2,1)S(1)}, u32[]{:S(2)}, u32[]{:S(2)}) collective-permute-start(bf16[1152,256]{1,0:T(8,128)(2,1)S(1)} %get-tuple-element.44), channel_id=1, source_target_pairs={{0,192},{8,200},{16,208},{24,216},{32,224},{40,232},{48,240},{56,2... | collective-permute-start | bytes 1769480 | tf_op jit(solution)/shard_map/ppermute | solution.py:26
  216.1 2.6 collective-permute-start.48
  218.7 3.2 collective-permute-start.27
  224.9 3.2 collective-permute-done.42.refs_7_
  229.0 3.7 collective-permute-start.25
  232.7 3.7 collective-permute-done.45.refs_10_
  238.4 2.3 collective-permute-done.48.refs_13_
  246.0 1.8 collective-permute-start.28
  252.4 2.7 collective-permute-start.30
  270.3 25.4 %attend.7 = (bf16[2048,256]{1,0:T(8,128)(2,1)}, f32[64,128]{1,0:T(8,128)S(1)}) custom-call(s32[64]{0:T(128)S(1)} %reshape.15.slot_ref, bf16[2048,512]{1,0:T(8,128)(2,1)S(1)} %copy-done.2, bf16[384,256]{1,0:T(8,128)(2,1)S(1)} %copy-done.37, bf16[384,256]{1,0:T(8,128)(2,1)S(1)} %copy-done.40, bf16[384,256]{1,0:T(8,128)(2,1)S(1)} %copy-done.54, ...), custom_call_target="tpu_custom_call" | custom-call | flops 268435456 | bytes 10485760 | tf_op jit(solution)/shard_map/attend/pallas_call | solution.py:208
  296.0 24.4 %attend.5 = (bf16[2048,256]{1,0:T(8,128)(2,1)}, f32[64,128]{1,0:T(8,128)S(1)}) custom-call(s32[64]{0:T(128)S(1)} %reshape.15.slot_ref, bf16[2048,512]{1,0:T(8,128)(2,1)S(1)} %copy-done.3, bf16[384,256]{1,0:T(8,128)(2,1)S(1)} %copy-done.43, bf16[384,256]{1,0:T(8,128)(2,1)S(1)} %copy-done.45, bf16[384,256]{1,0:T(8,128)(2,1)S(1)} %copy-done.69, ...), custom_call_target="tpu_custom_call" | custom-call | flops 268435456 | bytes 10485760 | tf_op jit(solution)/shard_map/attend/pallas_call | solution.py:208
  320.4 2.1 collective-permute-start.34
  324.2 2.0 collective-permute-start.53
  337.4 23.6 %attend.4 = (bf16[2048,256]{1,0:T(8,128)(2,1)S(1)}, f32[64,128]{1,0:T(8,128)S(1)}) custom-call(s32[64]{0:T(128)S(1)} %reshape.12.slot_ref, bf16[2048,512]{1,0:T(8,128)(2,1)S(1)} %copy-done, bf16[384,256]{1,0:T(8,128)(2,1)S(1)} %copy-done.43, bf16[384,256]{1,0:T(8,128)(2,1)S(1)} %copy-done.46, bf16[384,256]{1,0:T(8,128)(2,1)S(1)} %copy-done.70, ...), custom_call_target="tpu_custom_call" | custom-call | flops 268435456 | bytes 10485760 | tf_op jit(solution)/shard_map/attend/pallas_call | solution.py:208
  361.1 24.6 %attend.6 = (bf16[2048,256]{1,0:T(8,128)(2,1)S(1)}, f32[64,128]{1,0:T(8,128)S(1)}) custom-call(s32[64]{0:T(128)S(1)} %reshape.12.slot_ref, bf16[2048,512]{1,0:T(8,128)(2,1)S(1)} %copy-done, bf16[384,256]{1,0:T(8,128)(2,1)S(1)} %copy-done.38, bf16[384,256]{1,0:T(8,128)(2,1)S(1)} %copy-done.41, bf16[384,256]{1,0:T(8,128)(2,1)S(1)} %copy-done.55, ...), custom_call_target="tpu_custom_call" | custom-call | flops 268435456 | bytes 10485760 | tf_op jit(solution)/shard_map/attend/pallas_call | solution.py:208
  385.7 4.0 merge.2.refs_0_
  389.7 4.0 merge.3
  (317 shorter events, 70.0 us)
Async XLA Ops:
  6.5 97.5 %all-gather.3.cloned.1.call-start = ((), (), s32[]{:S(2)}) async-start(), calls=%async_computation | async-start | bytes 7077888 | tf_op jit(solution)/shard_map/all_gather | solution.py:275
  8.8 10.9 %collective-permute-start = (bf16[3,16,4096]{2,1,0:T(8,128)(2,1)S(1)}, bf16[3,16,4096]{2,1,0:T(8,128)(2,1)S(1)}, u32[]{:S(2)}, u32[]{:S(2)}) collective-permute-start(bf16[3,16,4096]{2,1,0:T(8,128)(2,1)S(1)} %broadcast_select_fusion), channel_id=1, source_target_pairs={{0,64},{8,72},{16,80},{24,88},{32,96},{40,104},{48,112},{56,120},{... | collective-permute-start | bytes 1179656 | tf_op jit(solution)/shard_map/ppermute | solution.py:26
  23.8 11.0 %collective-permute-start.2 = (bf16[256,512]{1,0:T(8,128)(2,1)S(1)}, bf16[256,512]{1,0:T(8,128)(2,1)S(1)}, u32[]{:S(2)}, u32[]{:S(2)}) collective-permute-start(bf16[256,512]{1,0:T(8,128)(2,1)S(1)} %copy-done.78), channel_id=1, source_target_pairs={{0,8},{8,16},{16,24},{24,32},{32,40},{40,48},{48,56},{56,0},{64,72... | collective-permute-start | bytes 786440 | tf_op jit(solution)/shard_map/ppermute | solution.py:26
  35.0 18.8 %collective-permute-start.4 = (bf16[768,512]{1,0:T(8,128)(2,1)S(1)}, bf16[768,512]{1,0:T(8,128)(2,1)S(1)}, u32[]{:S(2)}, u32[]{:S(2)}) collective-permute-start(bf16[768,512]{1,0:T(8,128)(2,1)S(1)} %get-tuple-element.40), channel_id=1, source_target_pairs={{0,8},{8,16},{16,24},{24,32},{32,40},{40,48},{48,56},{56,0},{64,72... | collective-permute-start | bytes 2359304 | tf_op jit(solution)/shard_map/ppermute | solution.py:26
  35.0 18.7 %collective-permute-start.5 = (bf16[768,512]{1,0:T(8,128)(2,1)S(1)}, bf16[768,512]{1,0:T(8,128)(2,1)S(1)}, u32[]{:S(2)}, u32[]{:S(2)}) collective-permute-start(bf16[768,512]{1,0:T(8,128)(2,1)S(1)} %get-tuple-element.39), channel_id=1, source_target_pairs={{0,56},{8,0},{16,8},{24,16},{32,24},{40,32},{48,40},{56,48},{64,12... | collective-permute-start | bytes 2359304 | tf_op jit(solution)/shard_map/ppermute | solution.py:26
  53.7 17.9 %collective-permute-start.7 = (bf16[768,512]{1,0:T(8,128)(2,1)S(1)}, bf16[768,512]{1,0:T(8,128)(2,1)S(1)}, u32[]{:S(2)}, u32[]{:S(2)}) collective-permute-start(bf16[768,512]{1,0:T(8,128)(2,1)S(1)} %collective-permute-done.4.refs_5_), channel_id=1, source_target_pairs={{0,8},{8,16},{16,24},{24,32},{32,40},{40,48},{48,56},{56,0},{64,72... | collective-permute-start | bytes 2359304 | tf_op jit(solution)/shard_map/ppermute | solution.py:26
  53.8 18.0 %collective-permute-start.8 = (bf16[768,512]{1,0:T(8,128)(2,1)S(1)}, bf16[768,512]{1,0:T(8,128)(2,1)S(1)}, u32[]{:S(2)}, u32[]{:S(2)}) collective-permute-start(bf16[768,512]{1,0:T(8,128)(2,1)S(1)} %collective-permute-done.5.refs_6_), channel_id=1, source_target_pairs={{0,56},{8,0},{16,8},{24,16},{32,24},{40,32},{48,40},{56,48},{64,12... | collective-permute-start | bytes 2359304 | tf_op jit(solution)/shard_map/ppermute | solution.py:26
  57.0 34.4 %collective-permute-start.6 = (bf16[768,512]{1,0:T(8,128)(2,1)S(1)}, bf16[768,512]{1,0:T(8,128)(2,1)S(1)}, u32[]{:S(2)}, u32[]{:S(2)}) collective-permute-start(bf16[768,512]{1,0:T(8,128)(2,1)S(1)} %get-tuple-element.41), channel_id=1, source_target_pairs={{0,192},{8,200},{16,208},{24,216},{32,224},{40,232},{48,240},{56,2... | collective-permute-start | bytes 2359304 | tf_op jit(solution)/shard_map/ppermute | solution.py:26
  71.7 14.2 %collective-permute-start.10 = (bf16[640,512]{1,0:T(8,128)(2,1)S(1)}, bf16[640,512]{1,0:T(8,128)(2,1)S(1)}, u32[]{:S(2)}, u32[]{:S(2)}) collective-permute-start(bf16[640,512]{1,0:T(8,128)(2,1)S(1)} %slice.202), channel_id=1, source_target_pairs={{0,8},{8,16},{16,24},{24,32},{32,40},{40,48},{48,56},{56,0},{64,72... | collective-permute-start | bytes 1966088 | tf_op jit(solution)/shard_map/ppermute | solution.py:26
  71.9 14.7 %collective-permute-start.11 = (bf16[640,512]{1,0:T(8,128)(2,1)S(1)}, bf16[640,512]{1,0:T(8,128)(2,1)S(1)}, u32[]{:S(2)}, u32[]{:S(2)}) collective-permute-start(bf16[640,512]{1,0:T(8,128)(2,1)S(1)} %pad_maximum_fusion.8), channel_id=1, source_target_pairs={{0,56},{8,0},{16,8},{24,16},{32,24},{40,32},{48,40},{56,48},{64,12... | collective-permute-start | bytes 1966088 | tf_op jit(solution)/shard_map/ppermute | solution.py:26
  76.1 17.0 %collective-permute-start.9 = (bf16[512,512]{1,0:T(8,128)(2,1)}, bf16[512,512]{1,0:T(8,128)(2,1)S(1)}, u32[]{:S(2)}, u32[]{:S(2)}) collective-permute-start(bf16[512,512]{1,0:T(8,128)(2,1)} %pad_maximum_fusion.11), channel_id=1, source_target_pairs={{0,192},{8,200},{16,208},{24,216},{32,224},{40,232},{48,240},{56,2... | collective-permute-start | bytes 1572872 | tf_op jit(solution)/shard_map/ppermute | solution.py:26
  77.4 23.8 %collective-permute-start.12 = (bf16[512,512]{1,0:T(8,128)(2,1)}, bf16[512,512]{1,0:T(8,128)(2,1)}, u32[]{:S(2)}, u32[]{:S(2)}) collective-permute-start(bf16[512,512]{1,0:T(8,128)(2,1)} %pad_maximum_fusion.12), channel_id=1, source_target_pairs={{0,192},{8,200},{16,208},{24,216},{32,224},{40,232},{48,240},{56,2... | collective-permute-start | bytes 1572872 | tf_op jit(solution)/shard_map/ppermute | solution.py:26
  86.6 14.6 %collective-permute-start.13 = (bf16[256,512]{1,0:T(8,128)(2,1)}, bf16[256,512]{1,0:T(8,128)(2,1)S(1)}, u32[]{:S(2)}, u32[]{:S(2)}) collective-permute-start(bf16[256,512]{1,0:T(8,128)(2,1)} %slice.207), channel_id=1, source_target_pairs={{0,8},{8,16},{16,24},{24,32},{32,40},{40,48},{48,56},{56,0},{64,72... | collective-permute-start | bytes 786440 | tf_op jit(solution)/shard_map/ppermute | solution.py:26
  87.4 13.8 %collective-permute-start.14 = (bf16[256,512]{1,0:T(8,128)(2,1)}, bf16[256,512]{1,0:T(8,128)(2,1)}, u32[]{:S(2)}, u32[]{:S(2)}) collective-permute-start(bf16[256,512]{1,0:T(8,128)(2,1)} %slice.208), channel_id=1, source_target_pairs={{0,56},{8,0},{16,8},{24,16},{32,24},{40,32},{48,40},{56,48},{64,12... | collective-permute-start | bytes 786440 | tf_op jit(solution)/shard_map/ppermute | solution.py:26
  92.2 11.8 %collective-permute-start.15 = (bf16[256,512]{1,0:T(8,128)(2,1)}, bf16[256,512]{1,0:T(8,128)(2,1)}, u32[]{:S(2)}, u32[]{:S(2)}) collective-permute-start(bf16[256,512]{1,0:T(8,128)(2,1)} %pad_maximum_fusion.22), channel_id=1, source_target_pairs={{0,192},{8,200},{16,208},{24,216},{32,224},{40,232},{48,240},{56,2... | collective-permute-start | bytes 786440 | tf_op jit(solution)/shard_map/ppermute | solution.py:26
  116.9 14.4 %collective-permute-start.16 = (bf16[768,256]{1,0:T(8,128)(2,1)S(1)}, bf16[768,256]{1,0:T(8,128)(2,1)S(1)}, u32[]{:S(2)}, u32[]{:S(2)}) collective-permute-start(bf16[768,256]{1,0:T(8,128)(2,1)S(1)} %pad_maximum_fusion.16), channel_id=1, source_target_pairs={{0,64},{8,72},{16,80},{24,88},{32,96},{40,104},{48,112},{56,120},{... | collective-permute-start | bytes 1179656 | tf_op jit(solution)/shard_map/ppermute | solution.py:26
  132.0 11.9 %collective-permute-start.39 = (bf16[384,256]{1,0:T(8,128)(2,1)S(1)}, bf16[384,256]{1,0:T(8,128)(2,1)S(1)}, u32[]{:S(2)}, u32[]{:S(2)}) collective-permute-start(bf16[384,256]{1,0:T(8,128)(2,1)S(1)} %get-tuple-element.36.refs_1_), channel_id=1, source_target_pairs={{0,56},{8,0},{16,8},{24,16},{32,24},{40,32},{48,40},{56,48},{64,12... | collective-permute-start | bytes 589832 | tf_op jit(solution)/shard_map/ppermute | solution.py:26
  135.2 79.2 %collective-permute-start.33 = (bf16[2048,512]{1,0:T(8,128)(2,1)S(1)}, bf16[2048,512]{1,0:T(8,128)(2,1)S(1)}, u32[]{:S(2)}, u32[]{:S(2)}) collective-permute-start(bf16[2048,512]{1,0:T(8,128)(2,1)S(1)} %copy-done), channel_id=1, source_target_pairs={{0,64},{8,72},{16,80},{24,88},{32,96},{40,104},{48,112},{56,120},{... | collective-permute-start | bytes 6291464 | tf_op jit(solution)/shard_map/ppermute | solution.py:26
  135.2 21.3 %collective-permute-start.18 = (bf16[384,256]{1,0:T(8,128)(2,1)S(1)}, bf16[384,256]{1,0:T(8,128)(2,1)S(1)}, u32[]{:S(2)}, u32[]{:S(2)}) collective-permute-start(bf16[384,256]{1,0:T(8,128)(2,1)S(1)} %get-tuple-element.35.refs_1_), channel_id=1, source_target_pairs={{0,8},{8,16},{16,24},{24,32},{32,40},{40,48},{48,56},{56,0},{64,72... | collective-permute-start | bytes 589832 | tf_op jit(solution)/shard_map/ppermute | solution.py:26
  139.3 17.2 %collective-permute-start.19 = (bf16[384,256]{1,0:T(8,128)(2,1)S(1)}, bf16[384,256]{1,0:T(8,128)(2,1)S(1)}, u32[]{:S(2)}, u32[]{:S(2)}) collective-permute-start(bf16[384,256]{1,0:T(8,128)(2,1)S(1)} %get-tuple-element.35.refs_1_), channel_id=1, source_target_pairs={{0,56},{8,0},{16,8},{24,16},{32,24},{40,32},{48,40},{56,48},{64,12... | collective-permute-start | bytes 589832 | tf_op jit(solution)/shard_map/ppermute | solution.py:26
  144.6 15.9 %collective-permute-start.40 = (bf16[1152,256]{1,0:T(8,128)(2,1)S(1)}, bf16[1152,256]{1,0:T(8,128)(2,1)S(1)}, u32[]{:S(2)}, u32[]{:S(2)}) collective-permute-start(bf16[1152,256]{1,0:T(8,128)(2,1)S(1)} %get-tuple-element.43), channel_id=1, source_target_pairs={{0,8},{8,16},{16,24},{24,32},{32,40},{40,48},{48,56},{56,0},{64,72... | collective-permute-start | bytes 1769480 | tf_op jit(solution)/shard_map/ppermute | solution.py:26
  147.5 24.9 %collective-permute-start.41 = (bf16[1152,256]{1,0:T(8,128)(2,1)S(1)}, bf16[1152,256]{1,0:T(8,128)(2,1)S(1)}, u32[]{:S(2)}, u32[]{:S(2)}) collective-permute-start(bf16[1152,256]{1,0:T(8,128)(2,1)S(1)} %get-tuple-element.42), channel_id=1, source_target_pairs={{0,56},{8,0},{16,8},{24,16},{32,24},{40,32},{48,40},{56,48},{64,12... | collective-permute-start | bytes 1769480 | tf_op jit(solution)/shard_map/ppermute | solution.py:26
  157.2 17.5 %collective-permute-start.20 = (bf16[1152,256]{1,0:T(8,128)(2,1)S(1)}, bf16[1152,256]{1,0:T(8,128)(2,1)S(1)}, u32[]{:S(2)}, u32[]{:S(2)}) collective-permute-start(bf16[1152,256]{1,0:T(8,128)(2,1)S(1)} %get-tuple-element.50), channel_id=1, source_target_pairs={{0,8},{8,16},{16,24},{24,32},{32,40},{40,48},{48,56},{56,0},{64,72... | collective-permute-start | bytes 1769480 | tf_op jit(solution)/shard_map/ppermute | solution.py:26
  158.9 26.1 %collective-permute-start.21 = (bf16[1152,256]{1,0:T(8,128)(2,1)S(1)}, bf16[1152,256]{1,0:T(8,128)(2,1)S(1)}, u32[]{:S(2)}, u32[]{:S(2)}) collective-permute-start(bf16[1152,256]{1,0:T(8,128)(2,1)S(1)} %get-tuple-element.49), channel_id=1, source_target_pairs={{0,56},{8,0},{16,8},{24,16},{32,24},{40,32},{48,40},{56,48},{64,12... | collective-permute-start | bytes 1769480 | tf_op jit(solution)/shard_map/ppermute | solution.py:26
  160.5 26.9 %collective-permute-start.43 = (bf16[1152,256]{1,0:T(8,128)(2,1)S(1)}, bf16[1152,256]{1,0:T(8,128)(2,1)S(1)}, u32[]{:S(2)}, u32[]{:S(2)}) collective-permute-start(bf16[1152,256]{1,0:T(8,128)(2,1)S(1)} %collective-permute-done.40.refs_5_), channel_id=1, source_target_pairs={{0,8},{8,16},{16,24},{24,32},{32,40},{40,48},{48,56},{56,0},{64,72... | collective-permute-start | bytes 1769480 | tf_op jit(solution)/shard_map/ppermute | solution.py:26
  172.4 25.3 %collective-permute-start.44 = (bf16[1152,256]{1,0:T(8,128)(2,1)S(1)}, bf16[1152,256]{1,0:T(8,128)(2,1)S(1)}, u32[]{:S(2)}, u32[]{:S(2)}) collective-permute-start(bf16[1152,256]{1,0:T(8,128)(2,1)S(1)} %collective-permute-done.41.refs_6_), channel_id=1, source_target_pairs={{0,56},{8,0},{16,8},{24,16},{32,24},{40,32},{48,40},{56,48},{64,12... | collective-permute-start | bytes 1769480 | tf_op jit(solution)/shard_map/ppermute | solution.py:26
  174.7 24.1 %collective-permute-start.23 = (bf16[1152,256]{1,0:T(8,128)(2,1)S(1)}, bf16[1152,256]{1,0:T(8,128)(2,1)S(1)}, u32[]{:S(2)}, u32[]{:S(2)}) collective-permute-start(bf16[1152,256]{1,0:T(8,128)(2,1)S(1)} %collective-permute-done.20.refs_5_), channel_id=1, source_target_pairs={{0,8},{8,16},{16,24},{24,32},{32,40},{40,48},{48,56},{56,0},{64,72... | collective-permute-start | bytes 1769480 | tf_op jit(solution)/shard_map/ppermute | solution.py:26
  185.1 21.5 %collective-permute-start.24 = (bf16[1152,256]{1,0:T(8,128)(2,1)S(1)}, bf16[1152,256]{1,0:T(8,128)(2,1)S(1)}, u32[]{:S(2)}, u32[]{:S(2)}) collective-permute-start(bf16[1152,256]{1,0:T(8,128)(2,1)S(1)} %collective-permute-done.21.refs_6_), channel_id=1, source_target_pairs={{0,56},{8,0},{16,8},{24,16},{32,24},{40,32},{48,40},{56,48},{64,12... | collective-permute-start | bytes 1769480 | tf_op jit(solution)/shard_map/ppermute | solution.py:26
  187.4 27.2 %collective-permute-start.22 = (bf16[1152,256]{1,0:T(8,128)(2,1)S(1)}, bf16[1152,256]{1,0:T(8,128)(2,1)S(1)}, u32[]{:S(2)}, u32[]{:S(2)}) collective-permute-start(bf16[1152,256]{1,0:T(8,128)(2,1)S(1)} %get-tuple-element.51), channel_id=1, source_target_pairs={{0,192},{8,200},{16,208},{24,216},{32,224},{40,232},{48,240},{56,2... | collective-permute-start | bytes 1769480 | tf_op jit(solution)/shard_map/ppermute | solution.py:26
  197.7 18.4 %collective-permute-start.46 = (bf16[960,256]{1,0:T(8,128)(2,1)S(1)}, bf16[960,256]{1,0:T(8,128)(2,1)S(1)}, u32[]{:S(2)}, u32[]{:S(2)}) collective-permute-start(bf16[960,256]{1,0:T(8,128)(2,1)S(1)} %slice.228), channel_id=1, source_target_pairs={{0,8},{8,16},{16,24},{24,32},{32,40},{40,48},{48,56},{56,0},{64,72... | collective-permute-start | bytes 1474568 | tf_op jit(solution)/shard_map/ppermute | solution.py:26
  198.9 19.9 %collective-permute-start.47 = (bf16[960,256]{1,0:T(8,128)(2,1)S(1)}, bf16[960,256]{1,0:T(8,128)(2,1)S(1)}, u32[]{:S(2)}, u32[]{:S(2)}) collective-permute-start(bf16[960,256]{1,0:T(8,128)(2,1)S(1)} %pad_maximum_fusion.14), channel_id=1, source_target_pairs={{0,56},{8,0},{16,8},{24,16},{32,24},{40,32},{48,40},{56,48},{64,12... | collective-permute-start | bytes 1474568 | tf_op jit(solution)/shard_map/ppermute | solution.py:26
  210.1 18.1 %collective-permute-start.42 = (bf16[1152,256]{1,0:T(8,128)(2,1)S(1)}, bf16[1152,256]{1,0:T(8,128)(2,1)S(1)}, u32[]{:S(2)}, u32[]{:S(2)}) collective-permute-start(bf16[1152,256]{1,0:T(8,128)(2,1)S(1)} %get-tuple-element.44), channel_id=1, source_target_pairs={{0,192},{8,200},{16,208},{24,216},{32,224},{40,232},{48,240},{56,2... | collective-permute-start | bytes 1769480 | tf_op jit(solution)/shard_map/ppermute | solution.py:26
  214.5 22.0 %collective-permute-start.45 = (bf16[768,256]{1,0:T(8,128)(2,1)S(1)}, bf16[768,256]{1,0:T(8,128)(2,1)S(1)}, u32[]{:S(2)}, u32[]{:S(2)}) collective-permute-start(bf16[768,256]{1,0:T(8,128)(2,1)S(1)} %pad_maximum_fusion.20), channel_id=1, source_target_pairs={{0,192},{8,200},{16,208},{24,216},{32,224},{40,232},{48,240},{56,2... | collective-permute-start | bytes 1179656 | tf_op jit(solution)/shard_map/ppermute | solution.py:26
  215.5 27.4 %collective-permute-start.26 = (bf16[960,256]{1,0:T(8,128)(2,1)S(1)}, bf16[960,256]{1,0:T(8,128)(2,1)S(1)}, u32[]{:S(2)}, u32[]{:S(2)}) collective-permute-start(bf16[960,256]{1,0:T(8,128)(2,1)S(1)} %slice.215), channel_id=1, source_target_pairs={{0,8},{8,16},{16,24},{24,32},{32,40},{40,48},{48,56},{56,0},{64,72... | collective-permute-start | bytes 1474568 | tf_op jit(solution)/shard_map/ppermute | solution.py:26
  216.1 24.6 %collective-permute-start.48 = (bf16[768,256]{1,0:T(8,128)(2,1)S(1)}, bf16[768,256]{1,0:T(8,128)(2,1)S(1)}, u32[]{:S(2)}, u32[]{:S(2)}) collective-permute-start(bf16[768,256]{1,0:T(8,128)(2,1)S(1)} %pad_maximum_fusion.21), channel_id=1, source_target_pairs={{0,192},{8,200},{16,208},{24,216},{32,224},{40,232},{48,240},{56,2... | collective-permute-start | bytes 1179656 | tf_op jit(solution)/shard_map/ppermute | solution.py:26
  218.7 26.4 %collective-permute-start.27 = (bf16[960,256]{1,0:T(8,128)(2,1)S(1)}, bf16[960,256]{1,0:T(8,128)(2,1)S(1)}, u32[]{:S(2)}, u32[]{:S(2)}) collective-permute-start(bf16[960,256]{1,0:T(8,128)(2,1)S(1)} %pad_maximum_fusion.13), channel_id=1, source_target_pairs={{0,56},{8,0},{16,8},{24,16},{32,24},{40,32},{48,40},{56,48},{64,12... | collective-permute-start | bytes 1474568 | tf_op jit(solution)/shard_map/ppermute | solution.py:26
  229.0 66.7 %collective-permute-start.25 = (bf16[768,256]{1,0:T(8,128)(2,1)}, bf16[768,256]{1,0:T(8,128)(2,1)}, u32[]{:S(2)}, u32[]{:S(2)}) collective-permute-start(bf16[768,256]{1,0:T(8,128)(2,1)} %pad_maximum_fusion.17), channel_id=1, source_target_pairs={{0,192},{8,200},{16,208},{24,216},{32,224},{40,232},{48,240},{56,2... | collective-permute-start | bytes 1179656 | tf_op jit(solution)/shard_map/ppermute | solution.py:26
  237.2 14.6 %collective-permute-start.49 = (bf16[384,256]{1,0:T(8,128)(2,1)}, bf16[384,256]{1,0:T(8,128)(2,1)}, u32[]{:S(2)}, u32[]{:S(2)}) collective-permute-start(bf16[384,256]{1,0:T(8,128)(2,1)} %slice.233), channel_id=1, source_target_pairs={{0,8},{8,16},{16,24},{24,32},{32,40},{40,48},{48,56},{56,0},{64,72... | collective-permute-start | bytes 589832 | tf_op jit(solution)/shard_map/ppermute | solution.py:26
  241.4 10.9 %collective-permute-start.50 = (bf16[384,256]{1,0:T(8,128)(2,1)}, bf16[384,256]{1,0:T(8,128)(2,1)}, u32[]{:S(2)}, u32[]{:S(2)}) collective-permute-start(bf16[384,256]{1,0:T(8,128)(2,1)} %slice.234), channel_id=1, source_target_pairs={{0,56},{8,0},{16,8},{24,16},{32,24},{40,32},{48,40},{56,48},{64,12... | collective-permute-start | bytes 589832 | tf_op jit(solution)/shard_map/ppermute | solution.py:26
  243.0 12.1 %collective-permute-start.51 = (bf16[384,256]{1,0:T(8,128)(2,1)}, bf16[384,256]{1,0:T(8,128)(2,1)}, u32[]{:S(2)}, u32[]{:S(2)}) collective-permute-start(bf16[384,256]{1,0:T(8,128)(2,1)} %pad_maximum_fusion.24), channel_id=1, source_target_pairs={{0,192},{8,200},{16,208},{24,216},{32,224},{40,232},{48,240},{56,2... | collective-permute-start | bytes 589832 | tf_op jit(solution)/shard_map/ppermute | solution.py:26
  246.0 49.8 %collective-permute-start.28 = (bf16[768,256]{1,0:T(8,128)(2,1)}, bf16[768,256]{1,0:T(8,128)(2,1)}, u32[]{:S(2)}, u32[]{:S(2)}) collective-permute-start(bf16[768,256]{1,0:T(8,128)(2,1)} %pad_maximum_fusion.18), channel_id=1, source_target_pairs={{0,192},{8,200},{16,208},{24,216},{32,224},{40,232},{48,240},{56,2... | collective-permute-start | bytes 1179656 | tf_op jit(solution)/shard_map/ppermute | solution.py:26
  251.8 44.0 %collective-permute-start.29 = (bf16[384,256]{1,0:T(8,128)(2,1)}, bf16[384,256]{1,0:T(8,128)(2,1)}, u32[]{:S(2)}, u32[]{:S(2)}) collective-permute-start(bf16[384,256]{1,0:T(8,128)(2,1)} %slice.220), channel_id=1, source_target_pairs={{0,8},{8,16},{16,24},{24,32},{32,40},{40,48},{48,56},{56,0},{64,72... | collective-permute-start | bytes 589832 | tf_op jit(solution)/shard_map/ppermute | solution.py:26
  252.4 43.5 %collective-permute-start.30 = (bf16[384,256]{1,0:T(8,128)(2,1)}, bf16[384,256]{1,0:T(8,128)(2,1)}, u32[]{:S(2)}, u32[]{:S(2)}) collective-permute-start(bf16[384,256]{1,0:T(8,128)(2,1)} %slice.221), channel_id=1, source_target_pairs={{0,56},{8,0},{16,8},{24,16},{32,24},{40,32},{48,40},{56,48},{64,12... | collective-permute-start | bytes 589832 | tf_op jit(solution)/shard_map/ppermute | solution.py:26
  255.1 40.8 %collective-permute-start.31 = (bf16[384,256]{1,0:T(8,128)(2,1)}, bf16[384,256]{1,0:T(8,128)(2,1)}, u32[]{:S(2)}, u32[]{:S(2)}) collective-permute-start(bf16[384,256]{1,0:T(8,128)(2,1)} %pad_maximum_fusion.23), channel_id=1, source_target_pairs={{0,192},{8,200},{16,208},{24,216},{32,224},{40,232},{48,240},{56,2... | collective-permute-start | bytes 589832 | tf_op jit(solution)/shard_map/ppermute | solution.py:26
  295.7 90.0 %collective-permute-start.52 = (bf16[2048,256]{1,0:T(8,128)(2,1)}, bf16[2048,256]{1,0:T(8,128)(2,1)}, u32[]{:S(2)}, u32[]{:S(2)}) collective-permute-start(bf16[2048,256]{1,0:T(8,128)(2,1)} %get-tuple-element.26), channel_id=1, source_target_pairs={{0,64},{8,72},{16,80},{24,88},{32,96},{40,104},{48,112},{56,120},{... | collective-permute-start | bytes 3145736 | tf_op jit(solution)/shard_map/ppermute | solution.py:26
  320.4 69.2 %collective-permute-start.34 = (bf16[2048,256]{1,0:T(8,128)(2,1)}, bf16[2048,256]{1,0:T(8,128)(2,1)}, u32[]{:S(2)}, u32[]{:S(2)}) collective-permute-start(bf16[2048,256]{1,0:T(8,128)(2,1)} %get-tuple-element.22), channel_id=1, source_target_pairs={{0,64},{8,72},{16,80},{24,88},{32,96},{40,104},{48,112},{56,120},{... | collective-permute-start | bytes 3145736 | tf_op jit(solution)/shard_map/ppermute | solution.py:26
  324.1 65.6 %collective-permute-start.35 = (f32[64,128]{1,0:T(8,128)S(1)}, f32[64,128]{1,0:T(8,128)S(1)}, u32[]{:S(2)}, u32[]{:S(2)}) collective-permute-start(f32[64,128]{1,0:T(8,128)S(1)} %get-tuple-element.24), channel_id=1, source_target_pairs={{0,64},{8,72},{16,80},{24,88},{32,96},{40,104},{48,112},{56,120},{... | collective-permute-start | bytes 98312 | tf_op jit(solution)/shard_map/ppermute | solution.py:26
  324.2 61.5 %collective-permute-start.53 = (f32[64,128]{1,0:T(8,128)S(1)}, f32[64,128]{1,0:T(8,128)S(1)}, u32[]{:S(2)}, u32[]{:S(2)}) collective-permute-start(f32[64,128]{1,0:T(8,128)S(1)} %get-tuple-element.28), channel_id=1, source_target_pairs={{0,64},{8,72},{16,80},{24,88},{32,96},{40,104},{48,112},{56,120},{... | collective-permute-start | bytes 98312 | tf_op jit(solution)/shard_map/ppermute | solution.py:26
  (100 other events, 1226.4 us)
Sparse Core Ops, SparseCore 0:
  21.0 44.2 all-gather.2
